TPU v7x, 128 devices: a whole 4x4x4 slice. The times are simulated.
128 devices in a mesh: row: 16 (over x, y), col: 4 (over z), depth: 2 (over core).
Axes of the slice: x: 4, y: 4, z: 4, core: 2. Of those that a mesh axis runs over, the one named last changes fastest.
Arguments:
- p_blocks: float32 [160, 4, 6, 128, 128], P('row', 'col', 'depth'), may hold values from -0.125 to 0.125
- s_blocks: float32 [160, 4, 6, 128, 128], P('row', 'col'), may hold values from -6 to 6
- p_pattern: int32 [160, 4, 6], P('row'), may hold values from -1 to 159, as said below
- s_pattern: int32 [160, 4, 6], P(None, 'col'), may hold values from -1 to 159, as said below
Outputs:
- product: float32 [160, 4, 6, 128, 128], P('row', 'col', 'depth')
Inputs may be any that keep to these rules, and one draw needn't show every extreme that they name: `p_pattern`: in each row and group of slots the filled slots come first. Every block column belongs to one grid column, the same in both patterns, and appears only in that group of slots; the columns of a block row are distinct and lie within cyclic distance 10 of the row, modulo 160. Some block row fills all 6 slots of some group. `s_pattern`: as for p_pattern, with the same grid column for each block column.
All inputs are finite; a program needn't handle non-finite values.
Results may differ from a plain program's by a relative error of at most 0.0003.
Values sent between devices are 32-bit elements; how exact they have to be, the bound alone decides.
A program may use at most 128 MiB of HBM per device.

v0:
```python
import jax
import jax.numpy as jnp
from jax import lax
from jax.sharding import PartitionSpec as P

BS = 128
W = 10


def padded(value, sides, width):
    for axis, dim in sides:
        devices, length = (lax.axis_size(axis), value.shape[dim])
        up = [(i, (i + 1) % devices) for i in range(devices)]
        down = [(j, i) for i, j in up]
        last = lax.slice_in_dim(value, length - width, length, axis=dim)
        first = lax.slice_in_dim(value, 0, width, axis=dim)
        before = lax.ppermute(last, axis, up)
        after = lax.ppermute(first, axis, down)
        value = jnp.concatenate([before, value, after], axis=dim)
    return value


def make_folder(
    p_pattern, s_pattern, slabs, targets, slot_start, first_row, total_rows, group_slots
):
    block_rows = p_pattern.shape[0]
    slab_rows = slabs.shape[0]

    def add_groups(totals, shard_piece, first_group):
        count = shard_piece.shape[1]
        slots_here = shard_piece.shape[2]
        inner_count = count * slots_here
        inner_all = lax.dynamic_slice(
            p_pattern, (0, first_group, slot_start), (block_rows, count, slots_here)
        )
        inner_all = inner_all.reshape(block_rows, inner_count)
        left_all = shard_piece.reshape(block_rows, inner_count, BS, BS)
        safe_cols = jnp.maximum(inner_all, 0)
        s_rows = s_pattern[safe_cols, 0, :]
        matches = (
            (s_rows[:, :, None, :] == targets[:, None, :, None])
            & (targets >= 0)[:, None, :, None]
            & (inner_all >= 0)[:, :, None, None]
        )
        selector = matches.astype(shard_piece.dtype)
        offset_rows = (safe_cols - first_row + W) % total_rows
        local_rows = jnp.clip(jnp.where(inner_all >= 0, offset_rows, W), 0, slab_rows - 1)

        def one_slot(inner_index, running):
            left = lax.dynamic_index_in_dim(left_all, inner_index, 1, keepdims=False)
            rows_here = lax.dynamic_index_in_dim(local_rows, inner_index, 1, keepdims=False)
            weights = lax.dynamic_index_in_dim(selector, inner_index, 1, keepdims=False)
            slab = jnp.take(slabs, rows_here, axis=0, mode="clip")
            partial_value = jnp.einsum("rmn,rnq->rmq", left, slab, precision=lax.Precision.HIGHEST)
            partial_value = partial_value.reshape(block_rows, BS, group_slots, BS)
            for source in range(group_slots):
                running = (
                    running
                    + weights[:, None, :, source, None] * partial_value[:, :, source, None, :]
                )
            return running

        return lax.fori_loop(0, inner_count, one_slot, totals)

    return add_groups


def per_device(p_blocks, s_blocks, p_pattern, s_pattern):
    block_rows = p_blocks.shape[0]
    half_slots = p_blocks.shape[2]
    group_slots = s_blocks.shape[2]
    grid_row = lax.axis_index("row")
    grid_col = lax.axis_index("col")
    layer = lax.axis_index("depth")
    total_rows = block_rows * lax.axis_size("row")
    first_row = grid_row * block_rows
    extended = padded(s_blocks, (("row", 0),), W)
    slabs = jnp.transpose(extended[:, 0], (0, 2, 1, 3)).reshape(
        extended.shape[0], BS, group_slots * BS
    )
    own_targets = lax.dynamic_slice_in_dim(p_pattern, grid_col, 1, 1)[:, 0, :]
    folder = make_folder(
        p_pattern,
        s_pattern,
        slabs,
        own_targets,
        layer * half_slots,
        first_row,
        total_rows,
        group_slots,
    )
    initial = jnp.zeros((block_rows, BS, group_slots, BS), jnp.float32)
    partial_sum = folder(initial, lax.all_gather(p_blocks, "col", axis=1, tiled=True), jnp.int32(0))
    shares = lax.psum_scatter(partial_sum, "depth", scatter_dimension=2, tiled=True)
    result = jnp.transpose(shares, (0, 2, 1, 3))
    return result[:, None]


def solution(mesh):
    in_specs = (
        P("row", "col", "depth", None, None),
        P("row", "col", None, None, None),
        P("row", None, None),
        P(None, "col", None),
    )
    out_specs = P("row", "col", "depth", None, None)
    return jax.shard_map(
        per_device, mesh=mesh, in_specs=in_specs, out_specs=out_specs, check_vma=False
    )
```

profile of v0, /device:TPU:1, one launch (start us, length us, event | category | flops | bytes accessed | tf_op | source)
XLA Modules:
  0.0 530.6 jit_solution(4072251657246047158)
XLA Ops:
  7.3 5.5 %copy.67 = f32[10,1,6,128,128]{3,4,2,0,1:T(8,128)} copy(f32[10,1,6,128,128]{4,3,2,1,0:T(8,128)} %param.7) | data formatting | bytes 7864320 | tf_op args[1]
  12.8 2.1 collective-permute-start
  14.9 3.6 collective-permute-start.1
  20.9 82.5 %collective-permute-done = f32[10,1,6,128,128]{3,4,2,0,1:T(8,128)} collective-permute-done((f32[10,1,6,128,128]{3,4,2,0,1:T(8,128)}, f32[10,1,6,128,128]{3,4,2,0,1:T(8,128)}, u32[]{:S(2)}, u32[]{:S(2)}) %collective-permute-start) | collective-permute-done | bytes 3932192 | tf_op jit(solution)/shard_map/ppermute | solution.py:17
  103.5 10.1 %pad_maximum_fusion = f32[30,1,6,128,128]{3,4,2,0,1:T(8,128)} fusion(f32[10,1,6,128,128]{3,4,2,0,1:T(8,128)} %collective-permute-done.1, f32[10,1,6,128,128]{3,4,2,0,1:T(8,128)} %copy.67, f32[10,1,6,128,128]{3,4,2,0,1:T(8,128)} %collective-permute-done), kind=kLoop, calls=%fused_computation.28 | loop fusion | flops 5898240 | bytes 23592960 | tf_op jit(solution)/shard_map/concatenate | solution.py:19
  113.5 12.3 %copy.70 = f32[30,128,768]{2,1,0:T(8,128)} copy(f32[30,128,768]{1,2,0:T(8,128)} %bitcast.80) | data formatting | bytes 23592960
  125.9 7.4 %copy.65 = f32[10,4,3,128,128]{4,3,0,2,1:T(8,128)} copy(f32[10,4,3,128,128]{4,3,2,1,0:T(8,128)} %all-gather.2.cloned.1.call-done) | data formatting | bytes 15728640 | tf_op jit(solution)/shard_map/all_gather | solution.py:93
  133.3 349.1 %while.14 = (s32[]{:T(128)}, f32[10,128,6,128]{3,2,1,0:T(8,128)}, f32[10,12,6,6]{0,2,3,1:T(8,128)}, f32[10,12,128,128]{3,2,0,1:T(8,128)}, s32[10,12]{0,1:T(8,128...) while((s32[]{:T(128)}, f32[10,128,6,128]{3,2,1,0:T(8,128)}, ...), condition=%wide.region_1.2_spmd.clone, body=%wide.region_0.1_spmd.clone.sunk | while | flops 1522729984 | bytes 43924068 | solution.py:63
  133.3 7.1 %gather_fusion = f32[10,128,768]{2,1,0:T(8,128)} fusion(f32[30,128,768]{2,1,0:T(8,128)} %get-tuple-element.256, s32[1024]{0:T(1024)S(1)} %pad_clamp_fusion.2), kind=kCustom, calls=%fused_computation.clone.clone.1 | custom fusion | bytes 7864360 | tf_op jit(solution)/shard_map/while/body/eval_jaxpr/jit(_take)/gather | solution.py:53
  140.4 8.2 %fusion.21 = f32[10,128,768]{1,2,0:T(8,128)S(1)} fusion(f32[10,128,768]{2,1,0:T(8,128)} %gather_fusion, f32[10,12,128,128]{3,2,0,1:T(8,128)} %get-tuple-element.254, s32[]{:T(128)} %get-tuple-element.243), kind=kOutput, calls=%fused_computation.14.clone.1 | convolution fusion | flops 1509949440 | bytes 8520192 | tf_op jit(solution)/shard_map/while/body/eval_jaxpr/rmn,rnq->rmq/dot_general | solution.py:54
  148.6 1.4 slice_bitcast_fusion.14
  152.3 2.2 copy.99
  155.7 5.5 %fusion.22 = f32[10,128,6,128]{3,2,1,0:T(8,128)} fusion(f32[10,128,6,128]{3,2,1,0:T(8,128)} %get-tuple-element.244, f32[10,128,128]{2,1,0:T(8,128)S(1)} %copy.93, f32[10,6]{1,0:T(8,128)S(1)} %copy.94, f32[10,128,128]{2,1,0:T(8,128)S(1)} %copy.95, f32[10,6]{1,0:T(8,128)S(1)} %copy.96, f32[10,128,128]{2,1,0:T(8,128)S(1)} %copy.97, ...), kind=kLoop, calls=%fused_computation.7.clone.1 | loop fusion | flops 12779520 | bytes 11797921 | tf_op jit(solution)/shard_map/while/body/eval_jaxpr/add | solution.py:58
  161.2 7.1 %gather_fusion = f32[10,128,768]{2,1,0:T(8,128)} fusion(f32[30,128,768]{2,1,0:T(8,128)} %get-tuple-element.256, s32[1024]{0:T(1024)S(1)} %pad_clamp_fusion.2), kind=kCustom, calls=%fused_computation.clone.clone.1 | custom fusion | bytes 7864360 | tf_op jit(solution)/shard_map/while/body/eval_jaxpr/jit(_take)/gather | solution.py:53
  168.3 8.2 %fusion.21 = f32[10,128,768]{1,2,0:T(8,128)S(1)} fusion(f32[10,128,768]{2,1,0:T(8,128)} %gather_fusion, f32[10,12,128,128]{3,2,0,1:T(8,128)} %get-tuple-element.254, s32[]{:T(128)} %get-tuple-element.243), kind=kOutput, calls=%fused_computation.14.clone.1 | convolution fusion | flops 1509949440 | bytes 8520192 | tf_op jit(solution)/shard_map/while/body/eval_jaxpr/rmn,rnq->rmq/dot_general | solution.py:54
  176.5 1.4 slice_bitcast_fusion.14
  180.2 2.2 copy.99
  183.7 6.7 %fusion.22 = f32[10,128,6,128]{3,2,1,0:T(8,128)} fusion(f32[10,128,6,128]{3,2,1,0:T(8,128)} %get-tuple-element.244, f32[10,128,128]{2,1,0:T(8,128)S(1)} %copy.93, f32[10,6]{1,0:T(8,128)S(1)} %copy.94, f32[10,128,128]{2,1,0:T(8,128)S(1)} %copy.95, f32[10,6]{1,0:T(8,128)S(1)} %copy.96, f32[10,128,128]{2,1,0:T(8,128)S(1)} %copy.97, ...), kind=kLoop, calls=%fused_computation.7.clone.1 | loop fusion | flops 12779520 | bytes 11797921 | tf_op jit(solution)/shard_map/while/body/eval_jaxpr/add | solution.py:58
  190.4 7.1 %gather_fusion = f32[10,128,768]{2,1,0:T(8,128)} fusion(f32[30,128,768]{2,1,0:T(8,128)} %get-tuple-element.256, s32[1024]{0:T(1024)S(1)} %pad_clamp_fusion.2), kind=kCustom, calls=%fused_computation.clone.clone.1 | custom fusion | bytes 7864360 | tf_op jit(solution)/shard_map/while/body/eval_jaxpr/jit(_take)/gather | solution.py:53
  197.5 8.2 %fusion.21 = f32[10,128,768]{1,2,0:T(8,128)S(1)} fusion(f32[10,128,768]{2,1,0:T(8,128)} %gather_fusion, f32[10,12,128,128]{3,2,0,1:T(8,128)} %get-tuple-element.254, s32[]{:T(128)} %get-tuple-element.243), kind=kOutput, calls=%fused_computation.14.clone.1 | convolution fusion | flops 1509949440 | bytes 8520192 | tf_op jit(solution)/shard_map/while/body/eval_jaxpr/rmn,rnq->rmq/dot_general | solution.py:54
  205.7 1.4 slice_bitcast_fusion.14
  209.4 2.2 copy.99
  212.9 6.7 %fusion.22 = f32[10,128,6,128]{3,2,1,0:T(8,128)} fusion(f32[10,128,6,128]{3,2,1,0:T(8,128)} %get-tuple-element.244, f32[10,128,128]{2,1,0:T(8,128)S(1)} %copy.93, f32[10,6]{1,0:T(8,128)S(1)} %copy.94, f32[10,128,128]{2,1,0:T(8,128)S(1)} %copy.95, f32[10,6]{1,0:T(8,128)S(1)} %copy.96, f32[10,128,128]{2,1,0:T(8,128)S(1)} %copy.97, ...), kind=kLoop, calls=%fused_computation.7.clone.1 | loop fusion | flops 12779520 | bytes 11797921 | tf_op jit(solution)/shard_map/while/body/eval_jaxpr/add | solution.py:58
  219.6 7.1 %gather_fusion = f32[10,128,768]{2,1,0:T(8,128)} fusion(f32[30,128,768]{2,1,0:T(8,128)} %get-tuple-element.256, s32[1024]{0:T(1024)S(1)} %pad_clamp_fusion.2), kind=kCustom, calls=%fused_computation.clone.clone.1 | custom fusion | bytes 7864360 | tf_op jit(solution)/shard_map/while/body/eval_jaxpr/jit(_take)/gather | solution.py:53
  226.7 8.2 %fusion.21 = f32[10,128,768]{1,2,0:T(8,128)S(1)} fusion(f32[10,128,768]{2,1,0:T(8,128)} %gather_fusion, f32[10,12,128,128]{3,2,0,1:T(8,128)} %get-tuple-element.254, s32[]{:T(128)} %get-tuple-element.243), kind=kOutput, calls=%fused_computation.14.clone.1 | convolution fusion | flops 1509949440 | bytes 8520192 | tf_op jit(solution)/shard_map/while/body/eval_jaxpr/rmn,rnq->rmq/dot_general | solution.py:54
  238.6 2.2 copy.99
  242.1 6.7 %fusion.22 = f32[10,128,6,128]{3,2,1,0:T(8,128)} fusion(f32[10,128,6,128]{3,2,1,0:T(8,128)} %get-tuple-element.244, f32[10,128,128]{2,1,0:T(8,128)S(1)} %copy.93, f32[10,6]{1,0:T(8,128)S(1)} %copy.94, f32[10,128,128]{2,1,0:T(8,128)S(1)} %copy.95, f32[10,6]{1,0:T(8,128)S(1)} %copy.96, f32[10,128,128]{2,1,0:T(8,128)S(1)} %copy.97, ...), kind=kLoop, calls=%fused_computation.7.clone.1 | loop fusion | flops 12779520 | bytes 11797921 | tf_op jit(solution)/shard_map/while/body/eval_jaxpr/add | solution.py:58
  248.8 7.1 %gather_fusion = f32[10,128,768]{2,1,0:T(8,128)} fusion(f32[30,128,768]{2,1,0:T(8,128)} %get-tuple-element.256, s32[1024]{0:T(1024)S(1)} %pad_clamp_fusion.2), kind=kCustom, calls=%fused_computation.clone.clone.1 | custom fusion | bytes 7864360 | tf_op jit(solution)/shard_map/while/body/eval_jaxpr/jit(_take)/gather | solution.py:53
  255.9 8.2 %fusion.21 = f32[10,128,768]{1,2,0:T(8,128)S(1)} fusion(f32[10,128,768]{2,1,0:T(8,128)} %gather_fusion, f32[10,12,128,128]{3,2,0,1:T(8,128)} %get-tuple-element.254, s32[]{:T(128)} %get-tuple-element.243), kind=kOutput, calls=%fused_computation.14.clone.1 | convolution fusion | flops 1509949440 | bytes 8520192 | tf_op jit(solution)/shard_map/while/body/eval_jaxpr/rmn,rnq->rmq/dot_general | solution.py:54
  267.8 2.2 copy.99
  271.3 6.7 %fusion.22 = f32[10,128,6,128]{3,2,1,0:T(8,128)} fusion(f32[10,128,6,128]{3,2,1,0:T(8,128)} %get-tuple-element.244, f32[10,128,128]{2,1,0:T(8,128)S(1)} %copy.93, f32[10,6]{1,0:T(8,128)S(1)} %copy.94, f32[10,128,128]{2,1,0:T(8,128)S(1)} %copy.95, f32[10,6]{1,0:T(8,128)S(1)} %copy.96, f32[10,128,128]{2,1,0:T(8,128)S(1)} %copy.97, ...), kind=kLoop, calls=%fused_computation.7.clone.1 | loop fusion | flops 12779520 | bytes 11797921 | tf_op jit(solution)/shard_map/while/body/eval_jaxpr/add | solution.py:58
  278.0 7.1 %gather_fusion = f32[10,128,768]{2,1,0:T(8,128)} fusion(f32[30,128,768]{2,1,0:T(8,128)} %get-tuple-element.256, s32[1024]{0:T(1024)S(1)} %pad_clamp_fusion.2), kind=kCustom, calls=%fused_computation.clone.clone.1 | custom fusion | bytes 7864360 | tf_op jit(solution)/shard_map/while/body/eval_jaxpr/jit(_take)/gather | solution.py:53
  285.1 8.2 %fusion.21 = f32[10,128,768]{1,2,0:T(8,128)S(1)} fusion(f32[10,128,768]{2,1,0:T(8,128)} %gather_fusion, f32[10,12,128,128]{3,2,0,1:T(8,128)} %get-tuple-element.254, s32[]{:T(128)} %get-tuple-element.243), kind=kOutput, calls=%fused_computation.14.clone.1 | convolution fusion | flops 1509949440 | bytes 8520192 | tf_op jit(solution)/shard_map/while/body/eval_jaxpr/rmn,rnq->rmq/dot_general | solution.py:54
  293.3 1.4 slice_bitcast_fusion.14
  297.0 2.2 copy.99
  300.5 6.7 %fusion.22 = f32[10,128,6,128]{3,2,1,0:T(8,128)} fusion(f32[10,128,6,128]{3,2,1,0:T(8,128)} %get-tuple-element.244, f32[10,128,128]{2,1,0:T(8,128)S(1)} %copy.93, f32[10,6]{1,0:T(8,128)S(1)} %copy.94, f32[10,128,128]{2,1,0:T(8,128)S(1)} %copy.95, f32[10,6]{1,0:T(8,128)S(1)} %copy.96, f32[10,128,128]{2,1,0:T(8,128)S(1)} %copy.97, ...), kind=kLoop, calls=%fused_computation.7.clone.1 | loop fusion | flops 12779520 | bytes 11797921 | tf_op jit(solution)/shard_map/while/body/eval_jaxpr/add | solution.py:58
  307.2 7.1 %gather_fusion = f32[10,128,768]{2,1,0:T(8,128)} fusion(f32[30,128,768]{2,1,0:T(8,128)} %get-tuple-element.256, s32[1024]{0:T(1024)S(1)} %pad_clamp_fusion.2), kind=kCustom, calls=%fused_computation.clone.clone.1 | custom fusion | bytes 7864360 | tf_op jit(solution)/shard_map/while/body/eval_jaxpr/jit(_take)/gather | solution.py:53
  314.3 8.2 %fusion.21 = f32[10,128,768]{1,2,0:T(8,128)S(1)} fusion(f32[10,128,768]{2,1,0:T(8,128)} %gather_fusion, f32[10,12,128,128]{3,2,0,1:T(8,128)} %get-tuple-element.254, s32[]{:T(128)} %get-tuple-element.243), kind=kOutput, calls=%fused_computation.14.clone.1 | convolution fusion | flops 1509949440 | bytes 8520192 | tf_op jit(solution)/shard_map/while/body/eval_jaxpr/rmn,rnq->rmq/dot_general | solution.py:54
  326.2 2.2 copy.99
  329.6 6.7 %fusion.22 = f32[10,128,6,128]{3,2,1,0:T(8,128)} fusion(f32[10,128,6,128]{3,2,1,0:T(8,128)} %get-tuple-element.244, f32[10,128,128]{2,1,0:T(8,128)S(1)} %copy.93, f32[10,6]{1,0:T(8,128)S(1)} %copy.94, f32[10,128,128]{2,1,0:T(8,128)S(1)} %copy.95, f32[10,6]{1,0:T(8,128)S(1)} %copy.96, f32[10,128,128]{2,1,0:T(8,128)S(1)} %copy.97, ...), kind=kLoop, calls=%fused_computation.7.clone.1 | loop fusion | flops 12779520 | bytes 11797921 | tf_op jit(solution)/shard_map/while/body/eval_jaxpr/add | solution.py:58
  336.4 7.1 %gather_fusion = f32[10,128,768]{2,1,0:T(8,128)} fusion(f32[30,128,768]{2,1,0:T(8,128)} %get-tuple-element.256, s32[1024]{0:T(1024)S(1)} %pad_clamp_fusion.2), kind=kCustom, calls=%fused_computation.clone.clone.1 | custom fusion | bytes 7864360 | tf_op jit(solution)/shard_map/while/body/eval_jaxpr/jit(_take)/gather | solution.py:53
  343.5 8.2 %fusion.21 = f32[10,128,768]{1,2,0:T(8,128)S(1)} fusion(f32[10,128,768]{2,1,0:T(8,128)} %gather_fusion, f32[10,12,128,128]{3,2,0,1:T(8,128)} %get-tuple-element.254, s32[]{:T(128)} %get-tuple-element.243), kind=kOutput, calls=%fused_computation.14.clone.1 | convolution fusion | flops 1509949440 | bytes 8520192 | tf_op jit(solution)/shard_map/while/body/eval_jaxpr/rmn,rnq->rmq/dot_general | solution.py:54
  351.7 1.4 slice_bitcast_fusion.14
  355.4 2.2 copy.99
  358.8 6.7 %fusion.22 = f32[10,128,6,128]{3,2,1,0:T(8,128)} fusion(f32[10,128,6,128]{3,2,1,0:T(8,128)} %get-tuple-element.244, f32[10,128,128]{2,1,0:T(8,128)S(1)} %copy.93, f32[10,6]{1,0:T(8,128)S(1)} %copy.94, f32[10,128,128]{2,1,0:T(8,128)S(1)} %copy.95, f32[10,6]{1,0:T(8,128)S(1)} %copy.96, f32[10,128,128]{2,1,0:T(8,128)S(1)} %copy.97, ...), kind=kLoop, calls=%fused_computation.7.clone.1 | loop fusion | flops 12779520 | bytes 11797921 | tf_op jit(solution)/shard_map/while/body/eval_jaxpr/add | solution.py:58
  365.6 7.1 %gather_fusion = f32[10,128,768]{2,1,0:T(8,128)} fusion(f32[30,128,768]{2,1,0:T(8,128)} %get-tuple-element.256, s32[1024]{0:T(1024)S(1)} %pad_clamp_fusion.2), kind=kCustom, calls=%fused_computation.clone.clone.1 | custom fusion | bytes 7864360 | tf_op jit(solution)/shard_map/while/body/eval_jaxpr/jit(_take)/gather | solution.py:53
  372.7 8.2 %fusion.21 = f32[10,128,768]{1,2,0:T(8,128)S(1)} fusion(f32[10,128,768]{2,1,0:T(8,128)} %gather_fusion, f32[10,12,128,128]{3,2,0,1:T(8,128)} %get-tuple-element.254, s32[]{:T(128)} %get-tuple-element.243), kind=kOutput, calls=%fused_computation.14.clone.1 | convolution fusion | flops 1509949440 | bytes 8520192 | tf_op jit(solution)/shard_map/while/body/eval_jaxpr/rmn,rnq->rmq/dot_general | solution.py:54
  384.6 2.2 copy.99
  388.0 6.7 %fusion.22 = f32[10,128,6,128]{3,2,1,0:T(8,128)} fusion(f32[10,128,6,128]{3,2,1,0:T(8,128)} %get-tuple-element.244, f32[10,128,128]{2,1,0:T(8,128)S(1)} %copy.93, f32[10,6]{1,0:T(8,128)S(1)} %copy.94, f32[10,128,128]{2,1,0:T(8,128)S(1)} %copy.95, f32[10,6]{1,0:T(8,128)S(1)} %copy.96, f32[10,128,128]{2,1,0:T(8,128)S(1)} %copy.97, ...), kind=kLoop, calls=%fused_computation.7.clone.1 | loop fusion | flops 12779520 | bytes 11797921 | tf_op jit(solution)/shard_map/while/body/eval_jaxpr/add | solution.py:58
  394.8 7.1 %gather_fusion = f32[10,128,768]{2,1,0:T(8,128)} fusion(f32[30,128,768]{2,1,0:T(8,128)} %get-tuple-element.256, s32[1024]{0:T(1024)S(1)} %pad_clamp_fusion.2), kind=kCustom, calls=%fused_computation.clone.clone.1 | custom fusion | bytes 7864360 | tf_op jit(solution)/shard_map/while/body/eval_jaxpr/jit(_take)/gather | solution.py:53
  401.9 8.2 %fusion.21 = f32[10,128,768]{1,2,0:T(8,128)S(1)} fusion(f32[10,128,768]{2,1,0:T(8,128)} %gather_fusion, f32[10,12,128,128]{3,2,0,1:T(8,128)} %get-tuple-element.254, s32[]{:T(128)} %get-tuple-element.243), kind=kOutput, calls=%fused_computation.14.clone.1 | convolution fusion | flops 1509949440 | bytes 8520192 | tf_op jit(solution)/shard_map/while/body/eval_jaxpr/rmn,rnq->rmq/dot_general | solution.py:54
  413.7 2.2 copy.99
  417.2 6.7 %fusion.22 = f32[10,128,6,128]{3,2,1,0:T(8,128)} fusion(f32[10,128,6,128]{3,2,1,0:T(8,128)} %get-tuple-element.244, f32[10,128,128]{2,1,0:T(8,128)S(1)} %copy.93, f32[10,6]{1,0:T(8,128)S(1)} %copy.94, f32[10,128,128]{2,1,0:T(8,128)S(1)} %copy.95, f32[10,6]{1,0:T(8,128)S(1)} %copy.96, f32[10,128,128]{2,1,0:T(8,128)S(1)} %copy.97, ...), kind=kLoop, calls=%fused_computation.7.clone.1 | loop fusion | flops 12779520 | bytes 11797921 | tf_op jit(solution)/shard_map/while/body/eval_jaxpr/add | solution.py:58
  424.0 7.1 %gather_fusion = f32[10,128,768]{2,1,0:T(8,128)} fusion(f32[30,128,768]{2,1,0:T(8,128)} %get-tuple-element.256, s32[1024]{0:T(1024)S(1)} %pad_clamp_fusion.2), kind=kCustom, calls=%fused_computation.clone.clone.1 | custom fusion | bytes 7864360 | tf_op jit(solution)/shard_map/while/body/eval_jaxpr/jit(_take)/gather | solution.py:53
  431.1 8.2 %fusion.21 = f32[10,128,768]{1,2,0:T(8,128)S(1)} fusion(f32[10,128,768]{2,1,0:T(8,128)} %gather_fusion, f32[10,12,128,128]{3,2,0,1:T(8,128)} %get-tuple-element.254, s32[]{:T(128)} %get-tuple-element.243), kind=kOutput, calls=%fused_computation.14.clone.1 | convolution fusion | flops 1509949440 | bytes 8520192 | tf_op jit(solution)/shard_map/while/body/eval_jaxpr/rmn,rnq->rmq/dot_general | solution.py:54
  442.9 2.2 copy.99
  446.4 6.7 %fusion.22 = f32[10,128,6,128]{3,2,1,0:T(8,128)} fusion(f32[10,128,6,128]{3,2,1,0:T(8,128)} %get-tuple-element.244, f32[10,128,128]{2,1,0:T(8,128)S(1)} %copy.93, f32[10,6]{1,0:T(8,128)S(1)} %copy.94, f32[10,128,128]{2,1,0:T(8,128)S(1)} %copy.95, f32[10,6]{1,0:T(8,128)S(1)} %copy.96, f32[10,128,128]{2,1,0:T(8,128)S(1)} %copy.97, ...), kind=kLoop, calls=%fused_computation.7.clone.1 | loop fusion | flops 12779520 | bytes 11797921 | tf_op jit(solution)/shard_map/while/body/eval_jaxpr/add | solution.py:58
  453.2 7.1 %gather_fusion = f32[10,128,768]{2,1,0:T(8,128)} fusion(f32[30,128,768]{2,1,0:T(8,128)} %get-tuple-element.256, s32[1024]{0:T(1024)S(1)} %pad_clamp_fusion.2), kind=kCustom, calls=%fused_computation.clone.clone.1 | custom fusion | bytes 7864360 | tf_op jit(solution)/shard_map/while/body/eval_jaxpr/jit(_take)/gather | solution.py:53
  460.3 8.2 %fusion.21 = f32[10,128,768]{1,2,0:T(8,128)S(1)} fusion(f32[10,128,768]{2,1,0:T(8,128)} %gather_fusion, f32[10,12,128,128]{3,2,0,1:T(8,128)} %get-tuple-element.254, s32[]{:T(128)} %get-tuple-element.243), kind=kOutput, calls=%fused_computation.14.clone.1 | convolution fusion | flops 1509949440 | bytes 8520192 | tf_op jit(solution)/shard_map/while/body/eval_jaxpr/rmn,rnq->rmq/dot_general | solution.py:54
  472.1 2.2 copy.99
  475.6 6.7 %fusion.22 = f32[10,128,6,128]{3,2,1,0:T(8,128)} fusion(f32[10,128,6,128]{3,2,1,0:T(8,128)} %get-tuple-element.244, f32[10,128,128]{2,1,0:T(8,128)S(1)} %copy.93, f32[10,6]{1,0:T(8,128)S(1)} %copy.94, f32[10,128,128]{2,1,0:T(8,128)S(1)} %copy.95, f32[10,6]{1,0:T(8,128)S(1)} %copy.96, f32[10,128,128]{2,1,0:T(8,128)S(1)} %copy.97, ...), kind=kLoop, calls=%fused_computation.7.clone.1 | loop fusion | flops 12779520 | bytes 11797921 | tf_op jit(solution)/shard_map/while/body/eval_jaxpr/add | solution.py:58
  482.3 5.0 copy.71
  488.7 32.0 %all-reduce.4.cloned.1.call-done = f32[10,128,6,128]{3,1,2,0:T(8,128)} async-done(((f32[10,128,6,128]{3,1,2,0:T(8,128)}), f32[10,128,6,128]{3,1,2,0:T(8,128)}) %all-reduce.4.cloned.1.call-update) | async-done | bytes 3932176
  520.7 3.0 dynamic-slice_bitcast_fusion.1
  (219 shorter events, 56.2 us)
Async XLA Ops:
  6.5 12.0 %copy-start = (s32[10,4,6]{0,1,2:T(4,128)S(1)}, s32[10,4,6]{0,1,2:T(4,128)}, u32[]{:S(2)}) copy-start(s32[10,4,6]{0,1,2:T(4,128)} %param.8) | copy-start | bytes 2884
  6.5 12.2 %copy-start.1 = (s32[160,1,6]{0,1,2:T(1,128)S(1)}, s32[160,1,6]{0,1,2:T(1,128)}, u32[]{:S(2)}) copy-start(s32[160,1,6]{0,1,2:T(1,128)} %param.9) | copy-start | bytes 11524
  6.5 119.3 %all-gather.2.cloned.1.call-start = ((), (), s32[]{:S(2)}) async-start(), calls=%async_computation | async-start | bytes 9830400 | tf_op jit(solution)/shard_map/all_gather | solution.py:93
  7.3 513.4 %all-reduce.4.cloned.1.call-start = ((), (), s32[]{:S(2)}) async-start(), calls=%async_computation.1 | async-start | bytes 7864320
  12.8 90.7 %collective-permute-start = (f32[10,1,6,128,128]{3,4,2,0,1:T(8,128)}, f32[10,1,6,128,128]{3,4,2,0,1:T(8,128)}, u32[]{:S(2)}, u32[]{:S(2)}) collective-permute-start(f32[10,1,6,128,128]{3,4,2,0,1:T(8,128)} %copy.67), channel_id=1, source_target_pairs={{0,8},{8,16},{16,24},{24,32},{32,40},{40,48},{48,56},{56,64},{64,7... | collective-permute-start | bytes 11796488 | tf_op jit(solution)/shard_map/ppermute | solution.py:17
  14.9 88.6 %collective-permute-start.1 = (f32[10,1,6,128,128]{3,4,2,0,1:T(8,128)}, f32[10,1,6,128,128]{3,4,2,0,1:T(8,128)}, u32[]{:S(2)}, u32[]{:S(2)}) collective-permute-start(f32[10,1,6,128,128]{3,4,2,0,1:T(8,128)} %copy.67), channel_id=1, source_target_pairs={{8,0},{16,8},{24,16},{32,24},{40,32},{48,40},{56,48},{64,56},{72,6... | collective-permute-start | bytes 11796488 | tf_op jit(solution)/shard_map/ppermute | solution.py:18
  482.3 5.1 copy-start.2
Sparse Core Ops, SparseCore 0:
  9.0 82.1 all-gather.1
  487.5 33.1 all-reduce.3
where the time goes:
time: 534 us; the launch traced here: 531 us
  local copies, waits for them, and re-layouts  206 us (39%)
  waiting for transfers between devices  115 us (22%)
  matrix products  98.5 us (18%)
  other arithmetic  90.5 us (17%)
  between operations  14.2 us (3%)
  starting transfers between devices  5.8 us (1%)
    dot_general x12, matrix products, one_slot(): jnp.einsum('rmn,rnq->rmq', left, slab, precision=lax.Precision.HIGHEST)  98.5 us
    gather x12, local copies, waits for them, and re-layouts, one_slot(): slab = jnp.take(slabs, rows_here, axis=0, mode='clip')  85.1 us
    ppermute x1, waiting for transfers between devices, padded(): before = lax.ppermute(last, axis, up)  82.5 us
    add x12, other arithmetic, one_slot(): running + weights[:, None, :, source, None] * partial_value[:, :, source,...  79.5 us
    mul x168, local copies, waits for them, and re-layouts, one_slot(): weights[:, None, :, source, None] * partial_value[:, :, source, None, :]  76.2 us
    unnamed x3, waiting for transfers between devices  32.8 us
    unnamed x11, local copies, waits for them, and re-layouts  18.5 us
  transfers between devices with their start and end apart: 4, of which 2 were waited for; matrix products, arithmetic and copies ran while one was open for 6% of the time, Pallas kernels for 0%

commit v1 on v0

v1 whole, which is shorter than its diff:
```python
import functools

import jax
import jax.numpy as jnp
from jax import lax
from jax.experimental import pallas as pl
from jax.experimental.pallas import tpu as pltpu
from jax.sharding import PartitionSpec as P

BS = 128
W = 10
MESH = pl.DeviceIdType.MESH
BF = jnp.bfloat16


def split(x):
    hi = x.astype(BF)
    return hi, (x - hi.astype(jnp.float32)).astype(BF)


def kernel(
    sizes,
    p_pat,
    s_pat,
    p_in,
    s_in,
    out,
    p_land,
    s_land,
    s_hi,
    s_lo,
    lhs,
    part,
    got,
    mine,
    table,
    p_send,
    p_recv,
    f_send,
    f_recv,
    s_send,
    s_recv,
    x_send,
    x_recv,
    e_send,
    e_recv,
    own_p,
    own_s,
    o_sem,
):
    n_row, n_col, rows, half = sizes
    slots = 2 * half
    total = n_row * rows
    window = 3 * rows
    zero_block = window * slots
    chunks = rows // 2
    r, z, d = lax.axis_index("row"), lax.axis_index("col"), lax.axis_index("depth")
    sib = 1 - d
    row_to = (lax.rem(r + 1, n_row), lax.rem(r + n_row - 1, n_row))
    col_to = (lax.rem(z + 1, n_col), lax.rem(z + n_col - 1, n_col))
    first_row = r * rows

    def p_direct(k, t):
        return pltpu.make_async_remote_copy(
            src_ref=p_in.at[t, 0],
            dst_ref=p_land.at[1 + k, t],
            send_sem=p_send.at[k, t],
            recv_sem=p_recv.at[k, t],
            device_id={"col": col_to[k]},
            device_id_type=MESH,
        )

    def p_forward(k, t):
        return pltpu.make_async_remote_copy(
            src_ref=p_land.at[1 + k, t],
            dst_ref=p_land.at[3, t],
            send_sem=f_send.at[t],
            recv_sem=f_recv.at[t],
            device_id={"col": col_to[k]},
            device_id_type=MESH,
        )

    def s_direct(k, u):
        at = d * chunks + u
        return pltpu.make_async_remote_copy(
            src_ref=s_in.at[at, 0],
            dst_ref=s_land.at[2 * k * rows + at],
            send_sem=s_send.at[k, u],
            recv_sem=s_recv.at[k, u],
            device_id={"row": row_to[k]},
            device_id_type=MESH,
        )

    def s_cross(k, u):
        at = 2 * k * rows + d * chunks + u
        return pltpu.make_async_remote_copy(
            src_ref=s_land.at[at],
            dst_ref=s_land.at[at],
            send_sem=x_send.at[k, u],
            recv_sem=x_recv.at[k, u],
            device_id={"depth": sib},
            device_id_type=MESH,
        )

    def exchange(i):
        return pltpu.make_async_remote_copy(
            src_ref=part.at[i],
            dst_ref=got.at[i],
            send_sem=e_send.at[i],
            recv_sem=e_recv.at[i],
            device_id={"depth": sib},
            device_id_type=MESH,
        )

    def load_s(t):
        return pltpu.make_async_copy(s_in.at[t, 0], s_land.at[rows + t], own_s.at[t])

    def load_p(t):
        return pltpu.make_async_copy(p_in.at[t, 0], p_land.at[0, t], own_p.at[t])

    def store(i):
        return pltpu.make_async_copy(mine.at[i], out.at[i, 0], o_sem.at[i])

    def convert(at):
        for b in range(slots):
            hi, lo = split(s_land[at, b])
            s_hi[at * slots + b] = hi
            s_lo[at * slots + b] = lo

    def index_row(i):
        for q, shift in enumerate((0, n_col - 1, 1, 2)):
            group = lax.rem(z + shift, n_col)
            for a in range(half):
                col = p_pat[(i * n_col + group) * slots + d * half + a]
                safe = jnp.maximum(col, 0)
                at = safe - first_row + W
                at = jnp.where(at < 0, at + total, at)
                at = jnp.where(at >= total, at - total, at)
                at = jnp.clip(at, 0, window - 1)
                have = [s_pat[safe * slots + b] for b in range(slots)]
                for c in range(slots):
                    target = p_pat[(i * n_col + z) * slots + lax.rem(c + d * half, slots)]
                    wanted = jnp.where(col >= 0, target, -1)
                    found = jnp.int32(zero_block)
                    for b in range(slots):
                        found = jnp.where(have[b] == wanted, at * slots + b, found)
                    found = jnp.where(wanted >= 0, found, zero_block)
                    table[(i * n_col * half + q * half + a) * slots + c] = found

    barrier = pltpu.get_barrier_semaphore()
    for k in range(2):
        pl.semaphore_signal(barrier, inc=1, device_id={"row": row_to[k]}, device_id_type=MESH)
        pl.semaphore_signal(barrier, inc=1, device_id={"col": col_to[k]}, device_id_type=MESH)
    pl.semaphore_signal(barrier, inc=1, device_id={"depth": sib}, device_id_type=MESH)
    pl.semaphore_wait(barrier, 5)

    @pl.loop(0, chunks)
    def _(u):
        for k in range(2):
            s_direct(k, u).start()
            for t in range(2):
                p_direct(k, 2 * u + t).start()

    @pl.loop(0, rows)
    def _(t):
        load_s(t).start()
        load_p(t).start()

    s_hi[zero_block] = jnp.zeros((BS, BS), BF)
    s_lo[zero_block] = jnp.zeros((BS, BS), BF)

    @pl.loop(0, chunks)
    def _(u):
        for t in range(2):
            index_row(2 * u + t)
            load_s(2 * u + t).wait()
            load_p(2 * u + t).wait()
            convert(rows + 2 * u + t)
        for t in range(2):
            for k in range(2):
                p_direct(k, 2 * u + t).wait_recv()
        for t in range(2):
            p_forward(t, 2 * u + t).start()
        for k in range(2):
            s_direct(k, u).wait_recv()
            s_cross(k, u).start()
        for k in range(2):
            convert(2 * k * rows + d * chunks + u)
        for k in range(2):
            s_cross(k, u).wait_recv()
            convert(2 * k * rows + sib * chunks + u)

    inner = n_col * half

    def finish(i):
        exchange(i).wait_recv()
        for c in range(half):
            mine[i, c] = mine[i, c] + got[i, c]
        store(i).start()

    @pl.loop(0, rows)
    def _(i):
        p_forward(0, i).wait_recv()
        for n in range(inner):
            hi, lo = split(p_land[n // half, i, n % half])
            lhs[0, :, n * BS : (n + 1) * BS] = hi
            lhs[1, :, n * BS : (n + 1) * BS] = lo
        for tile in reversed(range(slots // 2)):
            acc = jnp.zeros((BS, 2 * BS), jnp.float32)
            for pair in range(inner // 2):
                where = [
                    [
                        table[(i * inner + 2 * pair + n) * slots + 2 * tile + c]
                        for c in range(2)
                    ]
                    for n in range(2)
                ]

                def blocks(ref):
                    return jnp.concatenate(
                        [jnp.concatenate([ref[w] for w in line], axis=1) for line in where],
                        axis=0,
                    )

                cols = slice(2 * pair * BS, 2 * (pair + 1) * BS)
                right_hi, right_lo = blocks(s_hi), blocks(s_lo)
                acc += jnp.dot(lhs[0, :, cols], right_hi, preferred_element_type=jnp.float32)
                acc += jnp.dot(lhs[1, :, cols], right_hi, preferred_element_type=jnp.float32)
                acc += jnp.dot(lhs[0, :, cols], right_lo, preferred_element_type=jnp.float32)
            for c in range(2):
                slot = 2 * tile + c
                value = acc[:, c * BS : (c + 1) * BS]
                if slot < half:
                    mine[i, slot] = value
                else:
                    part[i, slot - half] = value
        exchange(i).start()

        @pl.when(i > 0)
        def _():
            finish(i - 1)

    finish(rows - 1)

    @pl.loop(0, rows)
    def _(i):
        store(i).wait()
        exchange(i).wait_send()
        p_forward(0, i).wait_send()
        for k in range(2):
            p_direct(k, i).wait_send()

    @pl.loop(0, chunks)
    def _(u):
        for k in range(2):
            s_direct(k, u).wait_send()
            s_cross(k, u).wait_send()


def per_device(p_blocks, s_blocks, p_pattern, s_pattern):
    rows, _, half = p_blocks.shape[:3]
    n_row, n_col = lax.axis_size("row"), lax.axis_size("col")
    slots = 2 * half
    f32 = jnp.float32
    dma = pltpu.SemaphoreType.DMA
    chunks = rows // 2
    return pl.pallas_call(
        functools.partial(kernel, (n_row, n_col, rows, half)),
        out_shape=jax.ShapeDtypeStruct(p_blocks.shape, f32),
        in_specs=[pl.BlockSpec(memory_space=pltpu.SMEM)] * 2
        + [pl.BlockSpec(memory_space=pl.ANY)] * 2,
        out_specs=pl.BlockSpec(memory_space=pl.ANY),
        scratch_shapes=[
            pltpu.VMEM((4, rows, half, BS, BS), f32),
            pltpu.VMEM((3 * rows, slots, BS, BS), f32),
            pltpu.VMEM((3 * rows * slots + 1, BS, BS), BF),
            pltpu.VMEM((3 * rows * slots + 1, BS, BS), BF),
            pltpu.VMEM((2, BS, n_col * half * BS), BF),
            pltpu.VMEM((rows, half, BS, BS), f32),
            pltpu.VMEM((rows, half, BS, BS), f32),
            pltpu.VMEM((rows, half, BS, BS), f32),
            pltpu.SMEM((rows * n_col * half * slots,), jnp.int32),
            dma((2, rows)),
            dma((2, rows)),
            dma((rows,)),
            dma((rows,)),
            dma((2, chunks)),
            dma((2, chunks)),
            dma((2, chunks)),
            dma((2, chunks)),
            dma((rows,)),
            dma((rows,)),
            dma((rows,)),
            dma((rows,)),
            dma((rows,)),
        ],
        compiler_params=pltpu.CompilerParams(
            collective_id=0, has_side_effects=True, vmem_limit_bytes=56 * 2**20
        ),
        cost_estimate=pl.CostEstimate(
            flops=9 * 10**9, bytes_accessed=10**7, transcendentals=0
        ),
    )(p_pattern.reshape(-1), s_pattern.reshape(-1), p_blocks, s_blocks)


def solution(mesh):
    in_specs = (
        P("row", "col", "depth", None, None),
        P("row", "col", None, None, None),
        P("row", None, None),
        P(None, "col", None),
    )
    out_specs = P("row", "col", "depth", None, None)
    return jax.shard_map(
        per_device, mesh=mesh, in_specs=in_specs, out_specs=out_specs, check_vma=False
    )
```

time: 534 us -> 86.9 us (0.16)
  local copies, waits for them, and re-layouts: 206 us -> 6.07 us
  waiting for transfers between devices: 115 us -> 0 us
  matrix products: 98.5 us -> 0 us
  other arithmetic: 90.5 us -> 0 us
  Pallas kernels: 0 us -> 80.6 us
  between operations: 14.2 us -> 0.02 us
  starting transfers between devices: 5.8 us -> 0 us
    dot_general x12 -> x0, matrix products: 98.5 us -> none  [one_slot(): jnp.einsum('rmn,rnq->rmq', left, slab, precision=lax.Precision.HIGHEST)]
    gather x16 -> x0, local copies, waits for them, and re-layouts: 86.3 us -> none  [the longest x12 85.1 us: one_slot(): slab = jnp.take(slabs, rows_here, axis=0, mode='clip')]
    ppermute x2 -> x0, waiting for transfers between devices: 82.5 us -> none  [the longest x1 82.5 us: padded(): before = lax.ppermute(last, axis, up)]
    pallas_call x0 -> x1, Pallas kernels: none -> 80.6 us  [per_device(): pl.pallas_call(functools.partial(kernel, (n_row, n_col, rows, half)), out...]
    add x12 -> x0, other arithmetic: 79.5 us -> none  [one_slot(): running + weights[:, None, :, source, None] * partial_value[:, :, source,...]
    mul x168 -> x0, local copies, waits for them, and re-layouts: 76.2 us -> none  [one_slot(): weights[:, None, :, source, None] * partial_value[:, :, source, None, :]]
    unnamed x3 -> x0, waiting for transfers between devices: 32.8 us -> none
    unnamed x11 -> x3, local copies, waits for them, and re-layouts: 18.5 us -> 4.62 us
  transfers between devices with their start and end apart: 4 -> 0, of which waited for: 2 -> 0; matrix products, arithmetic and copies ran while one was open for 6% -> 0% of each run, Pallas kernels for 0% -> 0%
where the time goes in v1:
time: 86.9 us; the launch traced here: 86.6 us
  Pallas kernels  80.6 us (93%)
  local copies, waits for them, and re-layouts  6.07 us (7%)
    pallas_call x1, Pallas kernels, per_device(): pl.pallas_call(functools.partial(kernel, (n_row, n_col, rows, half)), out...  80.6 us
    unnamed x3, local copies, waits for them, and re-layouts  4.62 us

profile of v1, /device:TPU:1, one launch (start us, length us, event | category | flops | bytes accessed | tf_op | source)
XLA Modules:
  0.0 86.6 jit_solution(9883085667479363295)
XLA Ops:
  0.0 0.8 copy.5
  0.8 0.7 reshape.6.p_pat
  1.5 0.8 copy.6
  2.3 0.7 reshape.7.s_pat
  3.1 80.6 %shard_map.46 = f32[10,1,3,128,128]{4,3,2,1,0:T(8,128)} custom-call(s32[240]{0:T(256)} %reshape.6.p_pat, s32[960]{0:T(1024)} %reshape.7.s_pat, f32[10,1,3,128,128]{4,3,2,1,0:T(8,128)} %p_in.1, f32[10,1,6,128,128]{4,3,2,1,0:T(8,128)} %s_in.1), custom_call_target="tpu_custom_call" | custom-call | flops 8999999488 | bytes 10000000 | tf_op jit(solution)/shard_map/pallas_call | solution.py:267
  83.6 3.0 %copy.8 = f32[10,1,3,128,128]{4,3,2,1,0:T(8,128)} copy(f32[10,1,3,128,128]{4,3,2,1,0:T(8,128)} %shard_map.46) | data formatting | bytes 3932160

commit v2 on v1

--- a/solution.py
+++ b/solution.py
@@ -20,19 +20,21 @@
 
 def kernel(
     sizes,
-    p_pat,
-    s_pat,
+    p_pat_in,
+    s_pat_in,
     p_in,
     s_in,
     out,
+    p_pat,
+    s_pat,
     p_land,
     s_land,
     s_hi,
     s_lo,
     lhs,
+    sums,
     part,
     got,
-    mine,
     table,
     p_send,
     p_recv,
@@ -46,7 +48,7 @@
     e_recv,
     own_p,
     own_s,
-    o_sem,
+    pat_sem,
 ):
     n_row, n_col, rows, half = sizes
     slots = 2 * half
@@ -71,11 +73,12 @@
         )
 
     def p_forward(k, t):
-        return pltpu.make_async_remote_copy(
-            src_ref=p_land.at[1 + k, t],
-            dst_ref=p_land.at[3, t],
-            send_sem=f_send.at[t],
-            recv_sem=f_recv.at[t],
+        piece = pl.ds(k * half * BS // 2, half * BS // 2)
+        return pltpu.make_async_remote_copy(
+            src_ref=p_land.at[1 + k, t, piece],
+            dst_ref=p_land.at[3, t, piece],
+            send_sem=f_send.at[k, t],
+            recv_sem=f_recv.at[k, t],
             device_id={"col": col_to[k]},
             device_id_type=MESH,
         )
@@ -118,9 +121,6 @@
     def load_p(t):
         return pltpu.make_async_copy(p_in.at[t, 0], p_land.at[0, t], own_p.at[t])
 
-    def store(i):
-        return pltpu.make_async_copy(mine.at[i], out.at[i, 0], o_sem.at[i])
-
     def convert(at):
         for b in range(slots):
             hi, lo = split(s_land[at, b])
@@ -131,15 +131,15 @@
         for q, shift in enumerate((0, n_col - 1, 1, 2)):
             group = lax.rem(z + shift, n_col)
             for a in range(half):
-                col = p_pat[(i * n_col + group) * slots + d * half + a]
+                col = p_pat[d * half + a, group, i]
                 safe = jnp.maximum(col, 0)
                 at = safe - first_row + W
                 at = jnp.where(at < 0, at + total, at)
                 at = jnp.where(at >= total, at - total, at)
                 at = jnp.clip(at, 0, window - 1)
-                have = [s_pat[safe * slots + b] for b in range(slots)]
+                have = [s_pat[b, 0, safe] for b in range(slots)]
                 for c in range(slots):
-                    target = p_pat[(i * n_col + z) * slots + lax.rem(c + d * half, slots)]
+                    target = p_pat[lax.rem(c + d * half, slots), z, i]
                     wanted = jnp.where(col >= 0, target, -1)
                     found = jnp.int32(zero_block)
                     for b in range(slots):
@@ -154,18 +154,30 @@
     pl.semaphore_signal(barrier, inc=1, device_id={"depth": sib}, device_id_type=MESH)
     pl.semaphore_wait(barrier, 5)
 
+    @pl.loop(0, rows)
+    def _(t):
+        for k in range(2):
+            p_direct(k, t).start()
+
     @pl.loop(0, chunks)
     def _(u):
         for k in range(2):
             s_direct(k, u).start()
-            for t in range(2):
-                p_direct(k, 2 * u + t).start()
+
+    patterns = [
+        pltpu.make_async_copy(p_pat_in, p_pat, pat_sem.at[0]),
+        pltpu.make_async_copy(s_pat_in, s_pat, pat_sem.at[1]),
+    ]
+    for copy in patterns:
+        copy.start()
 
     @pl.loop(0, rows)
     def _(t):
         load_s(t).start()
         load_p(t).start()
 
+    for copy in patterns:
+        copy.wait()
     s_hi[zero_block] = jnp.zeros((BS, BS), BF)
     s_lo[zero_block] = jnp.zeros((BS, BS), BF)
 
@@ -180,7 +192,8 @@
             for k in range(2):
                 p_direct(k, 2 * u + t).wait_recv()
         for t in range(2):
-            p_forward(t, 2 * u + t).start()
+            for k in range(2):
+                p_forward(k, 2 * u + t).start()
         for k in range(2):
             s_direct(k, u).wait_recv()
             s_cross(k, u).start()
@@ -195,66 +208,81 @@
     def finish(i):
         exchange(i).wait_recv()
         for c in range(half):
-            mine[i, c] = mine[i, c] + got[i, c]
-        store(i).start()
+            out[i, 0, c] = out[i, 0, c] + got[i, c]
+
+    early = 8
+
+    def spread(i, first, last):
+        for n in range(first, last):
+            block = slice(n % half * BS, (n % half + 1) * BS)
+            hi, lo = split(p_land[n // half, i, block])
+            lhs[0, :, n * BS : (n + 1) * BS] = hi
+            lhs[1, :, n * BS : (n + 1) * BS] = lo
+
+    def multiply(i, tile, first, last, acc):
+        for n in range(first, last, 2):
+            where = [
+                [table[(i * inner + m) * slots + 2 * tile + c] for c in range(2)]
+                for m in (n, n + 1)
+            ]
+
+            def blocks(ref):
+                return jnp.concatenate(
+                    [jnp.concatenate([ref[w] for w in line], axis=1) for line in where],
+                    axis=0,
+                )
+
+            cols = slice(n * BS, (n + 2) * BS)
+            right_hi, right_lo = blocks(s_hi), blocks(s_lo)
+            for left, right in ((0, right_hi), (1, right_hi), (0, right_lo)):
+                term = jnp.dot(
+                    lhs[left, :, cols], right, preferred_element_type=jnp.float32
+                )
+                acc = term if acc is None else acc + term
+        return acc
 
     @pl.loop(0, rows)
     def _(i):
-        p_forward(0, i).wait_recv()
-        for n in range(inner):
-            hi, lo = split(p_land[n // half, i, n % half])
-            lhs[0, :, n * BS : (n + 1) * BS] = hi
-            lhs[1, :, n * BS : (n + 1) * BS] = lo
+        spread(i, 0, 3 * half)
+        for tile in range(slots // 2):
+            sums[tile] = multiply(i, tile, 0, early, None)
+
+        @pl.when(i > 0)
+        def _():
+            finish(i - 1)
+
+        for k in range(2):
+            p_direct(k, i).wait_send()
+            p_forward(k, i).wait_recv()
+        spread(i, 3 * half, inner)
         for tile in reversed(range(slots // 2)):
-            acc = jnp.zeros((BS, 2 * BS), jnp.float32)
-            for pair in range(inner // 2):
-                where = [
-                    [
-                        table[(i * inner + 2 * pair + n) * slots + 2 * tile + c]
-                        for c in range(2)
-                    ]
-                    for n in range(2)
-                ]
-
-                def blocks(ref):
-                    return jnp.concatenate(
-                        [jnp.concatenate([ref[w] for w in line], axis=1) for line in where],
-                        axis=0,
-                    )
-
-                cols = slice(2 * pair * BS, 2 * (pair + 1) * BS)
-                right_hi, right_lo = blocks(s_hi), blocks(s_lo)
-                acc += jnp.dot(lhs[0, :, cols], right_hi, preferred_element_type=jnp.float32)
-                acc += jnp.dot(lhs[1, :, cols], right_hi, preferred_element_type=jnp.float32)
-                acc += jnp.dot(lhs[0, :, cols], right_lo, preferred_element_type=jnp.float32)
+            acc = multiply(i, tile, early, inner, sums[tile])
             for c in range(2):
                 slot = 2 * tile + c
                 value = acc[:, c * BS : (c + 1) * BS]
                 if slot < half:
-                    mine[i, slot] = value
+                    out[i, 0, slot] = value
                 else:
                     part[i, slot - half] = value
-        exchange(i).start()
+            if tile == half // 2:
+                exchange(i).start()
+
+        @pl.when(i < chunks)
+        def _():
+            for k in range(2):
+                s_direct(k, i).wait_send()
+                s_cross(k, i).wait_send()
 
         @pl.when(i > 0)
         def _():
-            finish(i - 1)
+            exchange(i - 1).wait_send()
+            for k in range(2):
+                p_forward(k, i - 1).wait_send()
 
     finish(rows - 1)
-
-    @pl.loop(0, rows)
-    def _(i):
-        store(i).wait()
-        exchange(i).wait_send()
-        p_forward(0, i).wait_send()
-        for k in range(2):
-            p_direct(k, i).wait_send()
-
-    @pl.loop(0, chunks)
-    def _(u):
-        for k in range(2):
-            s_direct(k, u).wait_send()
-            s_cross(k, u).wait_send()
+    exchange(rows - 1).wait_send()
+    for k in range(2):
+        p_forward(k, rows - 1).wait_send()
 
 
 def per_device(p_blocks, s_blocks, p_pattern, s_pattern):
@@ -266,24 +294,25 @@
     chunks = rows // 2
     return pl.pallas_call(
         functools.partial(kernel, (n_row, n_col, rows, half)),
-        out_shape=jax.ShapeDtypeStruct(p_blocks.shape, f32),
-        in_specs=[pl.BlockSpec(memory_space=pltpu.SMEM)] * 2
-        + [pl.BlockSpec(memory_space=pl.ANY)] * 2,
-        out_specs=pl.BlockSpec(memory_space=pl.ANY),
+        out_shape=pltpu.VMEM(p_blocks.shape, f32),
+        in_specs=[pl.BlockSpec(memory_space=pl.ANY)] * 4,
+        out_specs=pl.BlockSpec(memory_space=pltpu.VMEM),
         scratch_shapes=[
-            pltpu.VMEM((4, rows, half, BS, BS), f32),
+            pltpu.SMEM((slots, n_col, rows), jnp.int32),
+            pltpu.SMEM((slots, 1, n_row * rows), jnp.int32),
+            pltpu.VMEM((4, rows, half * BS, BS), f32),
             pltpu.VMEM((3 * rows, slots, BS, BS), f32),
             pltpu.VMEM((3 * rows * slots + 1, BS, BS), BF),
             pltpu.VMEM((3 * rows * slots + 1, BS, BS), BF),
             pltpu.VMEM((2, BS, n_col * half * BS), BF),
-            pltpu.VMEM((rows, half, BS, BS), f32),
+            pltpu.VMEM((half, BS, 2 * BS), f32),
             pltpu.VMEM((rows, half, BS, BS), f32),
             pltpu.VMEM((rows, half, BS, BS), f32),
             pltpu.SMEM((rows * n_col * half * slots,), jnp.int32),
             dma((2, rows)),
             dma((2, rows)),
-            dma((rows,)),
-            dma((rows,)),
+            dma((2, rows)),
+            dma((2, rows)),
             dma((2, chunks)),
             dma((2, chunks)),
             dma((2, chunks)),
@@ -292,7 +321,7 @@
             dma((rows,)),
             dma((rows,)),
             dma((rows,)),
-            dma((rows,)),
+            dma((2,)),
         ],
         compiler_params=pltpu.CompilerParams(
             collective_id=0, has_side_effects=True, vmem_limit_bytes=56 * 2**20
@@ -300,7 +329,12 @@
         cost_estimate=pl.CostEstimate(
             flops=9 * 10**9, bytes_accessed=10**7, transcendentals=0
         ),
-    )(p_pattern.reshape(-1), s_pattern.reshape(-1), p_blocks, s_blocks)
+    )(
+        jnp.transpose(p_pattern, (2, 1, 0)),
+        jnp.transpose(s_pattern, (2, 1, 0)),
+        p_blocks.reshape(rows, 1, half * BS, BS),
+        s_blocks,
+    )
 
 
 def solution(mesh):

time: 86.9 us -> 79.3 us (0.913)
  local copies, waits for them, and re-layouts: 6.07 us -> 1.27 us
  Pallas kernels: 80.6 us -> 77.9 us
    unnamed x3 -> x1, local copies, waits for them, and re-layouts: 4.62 us -> 1.27 us
    pallas_call x1, Pallas kernels: 80.6 us -> 77.9 us  [per_device(): pl.pallas_call(functools.partial(kernel, (n_row, n_col, rows, half)), out...]
    reshape x2 -> x0, local copies, waits for them, and re-layouts: 1.44 us -> none  [the longest x1 0.73 us: per_device(): s_pattern.reshape(-1)]
where the time goes in v2:
time: 79.3 us; the launch traced here: 79.1 us
  Pallas kernels  77.9 us (98%)
  local copies, waits for them, and re-layouts  1.27 us (2%)
    pallas_call x1, Pallas kernels, per_device(): pl.pallas_call(functools.partial(kernel, (n_row, n_col, rows, half)), out...  77.9 us

profile of v2, /device:TPU:1, one launch (start us, length us, event | category | flops | bytes accessed | tf_op | source)
XLA Modules:
  0.0 79.1 jit_solution(10785255952457764947)
XLA Ops:
  0.0 77.9 %shard_map.46 = f32[10,1,3,128,128]{4,3,2,1,0:T(8,128)S(1)} custom-call(s32[6,4,10]{2,1,0:T(4,128)} %bitcast.4, s32[6,1,160]{2,1,0:T(1,128)} %bitcast.5, f32[10,1,384,128]{3,2,1,0:T(8,128)} %bitcast.3, f32[10,1,6,128,128]{4,3,2,1,0:T(8,128)} %s_in.1), custom_call_target="tpu_custom_call" | custom-call | flops 8999999488 | bytes 10000000 | tf_op jit(solution)/shard_map/pallas_call | solution.py:295
  77.9 1.3 %copy.6 = f32[10,1,3,128,128]{4,3,2,1,0:T(8,128)} copy(f32[10,1,3,128,128]{4,3,2,1,0:T(8,128)S(1)} %shard_map.46) | data formatting | bytes 3932160

commit v3 on v2

--- a/solution.py
+++ b/solution.py
@@ -62,64 +62,76 @@
     col_to = (lax.rem(z + 1, n_col), lax.rem(z + n_col - 1, n_col))
     first_row = r * rows
 
-    def p_direct(k, t):
-        return pltpu.make_async_remote_copy(
-            src_ref=p_in.at[t, 0],
-            dst_ref=p_land.at[1 + k, t],
-            send_sem=p_send.at[k, t],
+    def p_direct(k, t, count=2):
+        return pltpu.make_async_remote_copy(
+            src_ref=p_in.at[pl.ds(2 * t, count)],
+            dst_ref=p_land.at[1 + k, pl.ds(2 * t, count)],
+            send_sem=p_send.at[k],
             recv_sem=p_recv.at[k, t],
             device_id={"col": col_to[k]},
             device_id_type=MESH,
         )
 
-    def p_forward(k, t):
-        piece = pl.ds(k * half * BS // 2, half * BS // 2)
-        return pltpu.make_async_remote_copy(
-            src_ref=p_land.at[1 + k, t, piece],
-            dst_ref=p_land.at[3, t, piece],
-            send_sem=f_send.at[k, t],
-            recv_sem=f_recv.at[k, t],
+    def p_forward(k, t, count=1):
+        lines = half * BS // 2
+        at = (pl.ds(t, count), pl.ds(k * lines, lines))
+        return pltpu.make_async_remote_copy(
+            src_ref=p_land.at[1 + k, *at],
+            dst_ref=p_land.at[3, *at],
+            send_sem=f_send.at[k],
+            recv_sem=f_recv.at[t],
             device_id={"col": col_to[k]},
             device_id_type=MESH,
         )
 
-    def s_direct(k, u):
+    def p_forwarded(t):
+        return pltpu.make_async_remote_copy(
+            src_ref=p_land.at[1, t],
+            dst_ref=p_land.at[3, t],
+            send_sem=f_send.at[0],
+            recv_sem=f_recv.at[t],
+            device_id={"col": col_to[0]},
+            device_id_type=MESH,
+        )
+
+    def s_direct(k, u, count=1):
         at = d * chunks + u
         return pltpu.make_async_remote_copy(
-            src_ref=s_in.at[at, 0],
-            dst_ref=s_land.at[2 * k * rows + at],
-            send_sem=s_send.at[k, u],
+            src_ref=s_in.at[pl.ds(at, count), 0],
+            dst_ref=s_land.at[pl.ds(2 * k * rows + at, count)],
+            send_sem=s_send.at[k],
             recv_sem=s_recv.at[k, u],
             device_id={"row": row_to[k]},
             device_id_type=MESH,
         )
 
-    def s_cross(k, u):
-        at = 2 * k * rows + d * chunks + u
+    def s_cross(k, u, count=1):
+        at = pl.ds(2 * k * rows + d * chunks + u, count)
         return pltpu.make_async_remote_copy(
             src_ref=s_land.at[at],
             dst_ref=s_land.at[at],
-            send_sem=x_send.at[k, u],
+            send_sem=x_send.at[k],
             recv_sem=x_recv.at[k, u],
             device_id={"depth": sib},
             device_id_type=MESH,
         )
 
-    def exchange(i):
-        return pltpu.make_async_remote_copy(
-            src_ref=part.at[i],
-            dst_ref=got.at[i],
-            send_sem=e_send.at[i],
+    def exchange(i, first=0, count=half, lines=1):
+        at = (pl.ds(i, lines), pl.ds(first, count))
+        return pltpu.make_async_remote_copy(
+            src_ref=part.at[*at],
+            dst_ref=got.at[*at],
+            send_sem=e_send,
             recv_sem=e_recv.at[i],
             device_id={"depth": sib},
             device_id_type=MESH,
         )
 
-    def load_s(t):
-        return pltpu.make_async_copy(s_in.at[t, 0], s_land.at[rows + t], own_s.at[t])
-
-    def load_p(t):
-        return pltpu.make_async_copy(p_in.at[t, 0], p_land.at[0, t], own_p.at[t])
+    def load_s(u):
+        at = pl.ds(2 * u, 2)
+        return pltpu.make_async_copy(
+            s_in.at[at, 0], s_land.at[pl.ds(rows + 2 * u, 2)], own_s.at[u]
+        )
 
     def convert(at):
         for b in range(slots):
@@ -154,15 +166,12 @@
     pl.semaphore_signal(barrier, inc=1, device_id={"depth": sib}, device_id_type=MESH)
     pl.semaphore_wait(barrier, 5)
 
-    @pl.loop(0, rows)
-    def _(t):
-        for k in range(2):
-            p_direct(k, t).start()
-
-    @pl.loop(0, chunks)
-    def _(u):
-        for k in range(2):
-            s_direct(k, u).start()
+    for start in (p_direct, s_direct):
+
+        @pl.loop(0, chunks)
+        def _(u):
+            for k in range(2):
+                start(k, u).start()
 
     patterns = [
         pltpu.make_async_copy(p_pat_in, p_pat, pat_sem.at[0]),
@@ -171,10 +180,12 @@
     for copy in patterns:
         copy.start()
 
-    @pl.loop(0, rows)
-    def _(t):
-        load_s(t).start()
-        load_p(t).start()
+    load_p = pltpu.make_async_copy(p_in, p_land.at[0], own_p)
+    load_p.start()
+
+    @pl.loop(0, chunks)
+    def _(u):
+        load_s(u).start()
 
     for copy in patterns:
         copy.wait()
@@ -185,12 +196,11 @@
     def _(u):
         for t in range(2):
             index_row(2 * u + t)
-            load_s(2 * u + t).wait()
-            load_p(2 * u + t).wait()
+        load_s(u).wait()
+        for t in range(2):
             convert(rows + 2 * u + t)
-        for t in range(2):
-            for k in range(2):
-                p_direct(k, 2 * u + t).wait_recv()
+        for k in range(2):
+            p_direct(k, u).wait_recv()
         for t in range(2):
             for k in range(2):
                 p_forward(k, 2 * u + t).start()
@@ -210,7 +220,8 @@
         for c in range(half):
             out[i, 0, c] = out[i, 0, c] + got[i, c]
 
-    early = 8
+    direct = 3 * half
+    load_p.wait()
 
     def spread(i, first, last):
         for n in range(first, last):
@@ -220,43 +231,50 @@
             lhs[1, :, n * BS : (n + 1) * BS] = lo
 
     def multiply(i, tile, first, last, acc):
-        for n in range(first, last, 2):
-            where = [
-                [table[(i * inner + m) * slots + 2 * tile + c] for c in range(2)]
-                for m in (n, n + 1)
-            ]
-
-            def blocks(ref):
-                return jnp.concatenate(
-                    [jnp.concatenate([ref[w] for w in line], axis=1) for line in where],
-                    axis=0,
-                )
-
-            cols = slice(n * BS, (n + 2) * BS)
-            right_hi, right_lo = blocks(s_hi), blocks(s_lo)
-            for left, right in ((0, right_hi), (1, right_hi), (0, right_lo)):
-                term = jnp.dot(
-                    lhs[left, :, cols], right, preferred_element_type=jnp.float32
-                )
-                acc = term if acc is None else acc + term
+        terms = [
+            (left, right, n)
+            for left, right in ((0, s_hi), (1, s_hi), (0, s_lo))
+            for n in range(first, last)
+        ]
+        for at in range(0, len(terms), 2):
+            pair = terms[at : at + 2]
+            wide = jnp.concatenate(
+                [lhs[left, :, n * BS : (n + 1) * BS] for left, _, n in pair], axis=1
+            )
+            deep = jnp.concatenate(
+                [
+                    jnp.concatenate(
+                        [
+                            right[table[(i * inner + n) * slots + 2 * tile + c]]
+                            for c in range(2)
+                        ],
+                        axis=1,
+                    )
+                    for _, right, n in pair
+                ],
+                axis=0,
+            )
+            term = jnp.dot(wide, deep, preferred_element_type=jnp.float32)
+            acc = term if acc is None else acc + term
         return acc
 
     @pl.loop(0, rows)
     def _(i):
-        spread(i, 0, 3 * half)
+        spread(i, 0, direct)
         for tile in range(slots // 2):
-            sums[tile] = multiply(i, tile, 0, early, None)
-
-        @pl.when(i > 0)
-        def _():
-            finish(i - 1)
-
-        for k in range(2):
-            p_direct(k, i).wait_send()
-            p_forward(k, i).wait_recv()
-        spread(i, 3 * half, inner)
+            sums[i, tile] = multiply(i, tile, 0, direct, None)
+
+    for k in range(2):
+        p_direct(k, 0, rows).wait_send()
+        s_direct(k, 0, chunks).wait_send()
+        s_cross(k, 0, chunks).wait_send()
+
+    @pl.loop(0, rows)
+    def _(i):
+        p_forwarded(i).wait_recv()
+        spread(i, direct, inner)
         for tile in reversed(range(slots // 2)):
-            acc = multiply(i, tile, early, inner, sums[tile])
+            acc = multiply(i, tile, direct, inner, sums[i, tile])
             for c in range(2):
                 slot = 2 * tile + c
                 value = acc[:, c * BS : (c + 1) * BS]
@@ -264,25 +282,19 @@
                     out[i, 0, slot] = value
                 else:
                     part[i, slot - half] = value
-            if tile == half // 2:
-                exchange(i).start()
-
-        @pl.when(i < chunks)
-        def _():
-            for k in range(2):
-                s_direct(k, i).wait_send()
-                s_cross(k, i).wait_send()
+            if tile == 2:
+                exchange(i, 1, 2).start()
+            if tile == 1:
+                exchange(i, 0, 1).start()
 
         @pl.when(i > 0)
         def _():
-            exchange(i - 1).wait_send()
-            for k in range(2):
-                p_forward(k, i - 1).wait_send()
-
+            finish(i - 1)
+
+    for k in range(2):
+        p_forward(k, 0, rows).wait_send()
     finish(rows - 1)
-    exchange(rows - 1).wait_send()
-    for k in range(2):
-        p_forward(k, rows - 1).wait_send()
+    exchange(0, lines=rows).wait_send()
 
 
 def per_device(p_blocks, s_blocks, p_pattern, s_pattern):
@@ -305,22 +317,22 @@
             pltpu.VMEM((3 * rows * slots + 1, BS, BS), BF),
             pltpu.VMEM((3 * rows * slots + 1, BS, BS), BF),
             pltpu.VMEM((2, BS, n_col * half * BS), BF),
-            pltpu.VMEM((half, BS, 2 * BS), f32),
+            pltpu.VMEM((rows, half, BS, 2 * BS), f32),
             pltpu.VMEM((rows, half, BS, BS), f32),
             pltpu.VMEM((rows, half, BS, BS), f32),
             pltpu.SMEM((rows * n_col * half * slots,), jnp.int32),
-            dma((2, rows)),
-            dma((2, rows)),
-            dma((2, rows)),
-            dma((2, rows)),
+            dma((2,)),
             dma((2, chunks)),
+            dma((2,)),
+            dma((rows,)),
+            dma((2,)),
             dma((2, chunks)),
+            dma((2,)),
             dma((2, chunks)),
-            dma((2, chunks)),
+            dma,
             dma((rows,)),
-            dma((rows,)),
-            dma((rows,)),
-            dma((rows,)),
+            dma,
+            dma((chunks,)),
             dma((2,)),
         ],
         compiler_params=pltpu.CompilerParams(
@@ -332,7 +344,7 @@
     )(
         jnp.transpose(p_pattern, (2, 1, 0)),
         jnp.transpose(s_pattern, (2, 1, 0)),
-        p_blocks.reshape(rows, 1, half * BS, BS),
+        p_blocks.reshape(rows, half * BS, BS),
         s_blocks,
     )
 

time: 79.3 us -> 78 us (0.984)
  Pallas kernels: 77.9 us -> 76.5 us
    pallas_call x1, Pallas kernels: 77.9 us -> 76.5 us  [per_device(): pl.pallas_call(functools.partial(kernel, (n_row, n_col, rows, half)), out...]
where the time goes in v3:
time: 78 us; the launch traced here: 77.8 us
  Pallas kernels  76.5 us (98%)
  local copies, waits for them, and re-layouts  1.27 us (2%)
    pallas_call x1, Pallas kernels, per_device(): pl.pallas_call(functools.partial(kernel, (n_row, n_col, rows, half)), out...  76.5 us

profile of v3, /device:TPU:1, one launch (start us, length us, event | category | flops | bytes accessed | tf_op | source)
XLA Modules:
  0.0 77.8 jit_solution(9188044633499267235)
XLA Ops:
  0.0 76.5 %shard_map.46 = f32[10,1,3,128,128]{4,3,2,1,0:T(8,128)S(1)} custom-call(s32[6,4,10]{2,1,0:T(4,128)} %bitcast.4, s32[6,1,160]{2,1,0:T(1,128)} %bitcast.5, f32[10,384,128]{2,1,0:T(8,128)} %bitcast.3, f32[10,1,6,128,128]{4,3,2,1,0:T(8,128)} %s_in.1), custom_call_target="tpu_custom_call" | custom-call | flops 8999999488 | bytes 10000000 | tf_op jit(solution)/shard_map/pallas_call | solution.py:307
  76.5 1.3 %copy.6 = f32[10,1,3,128,128]{4,3,2,1,0:T(8,128)} copy(f32[10,1,3,128,128]{4,3,2,1,0:T(8,128)S(1)} %shard_map.46) | data formatting | bytes 3932160

commit v4 on v3

--- a/solution.py
+++ b/solution.py
@@ -199,11 +199,16 @@
         load_s(u).wait()
         for t in range(2):
             convert(rows + 2 * u + t)
+
+    def pass_on(u):
         for k in range(2):
             p_direct(k, u).wait_recv()
         for t in range(2):
             for k in range(2):
                 p_forward(k, 2 * u + t).start()
+
+    @pl.loop(0, chunks)
+    def _(u):
         for k in range(2):
             s_direct(k, u).wait_recv()
             s_cross(k, u).start()
@@ -212,6 +217,10 @@
         for k in range(2):
             s_cross(k, u).wait_recv()
             convert(2 * k * rows + sib * chunks + u)
+
+        @pl.when(u < chunks - 1)
+        def _():
+            pass_on(u)
 
     inner = n_col * half
 
@@ -258,19 +267,12 @@
             acc = term if acc is None else acc + term
         return acc
 
-    @pl.loop(0, rows)
-    def _(i):
+    def begin(i):
         spread(i, 0, direct)
         for tile in range(slots // 2):
             sums[i, tile] = multiply(i, tile, 0, direct, None)
 
-    for k in range(2):
-        p_direct(k, 0, rows).wait_send()
-        s_direct(k, 0, chunks).wait_send()
-        s_cross(k, 0, chunks).wait_send()
-
-    @pl.loop(0, rows)
-    def _(i):
+    def complete(i):
         p_forwarded(i).wait_recv()
         spread(i, direct, inner)
         for tile in reversed(range(slots // 2)):
@@ -287,9 +289,30 @@
             if tile == 1:
                 exchange(i, 0, 1).start()
 
-        @pl.when(i > 0)
-        def _():
-            finish(i - 1)
+    @pl.loop(0, rows + 1)
+    def _(j):
+        @pl.when(j == 5)
+        def _():
+            pass_on(chunks - 1)
+
+        @pl.when(j < rows)
+        def _():
+            begin(j)
+
+        @pl.when(j == rows - 1)
+        def _():
+            for k in range(2):
+                p_direct(k, 0, rows).wait_send()
+                s_direct(k, 0, chunks).wait_send()
+                s_cross(k, 0, chunks).wait_send()
+
+        @pl.when(j > 0)
+        def _():
+            complete(j - 1)
+
+        @pl.when(j > 1)
+        def _():
+            finish(j - 2)
 
     for k in range(2):
         p_forward(k, 0, rows).wait_send()

time: 78 us -> 78 us (level)
  no operation moved by 1% of the time
where the time goes in v4:
time: 78 us; the launch traced here: 77.8 us
  Pallas kernels  76.5 us (98%)
  local copies, waits for them, and re-layouts  1.27 us (2%)
    pallas_call x1, Pallas kernels, per_device(): pl.pallas_call(functools.partial(kernel, (n_row, n_col, rows, half)), out...  76.5 us

profile of v4, /device:TPU:1, one launch (start us, length us, event | category | flops | bytes accessed | tf_op | source)
XLA Modules:
  0.0 77.8 jit_solution(734649912159742416)
XLA Ops:
  0.0 76.5 %shard_map.46 = f32[10,1,3,128,128]{4,3,2,1,0:T(8,128)S(1)} custom-call(s32[6,4,10]{2,1,0:T(4,128)} %bitcast.4, s32[6,1,160]{2,1,0:T(1,128)} %bitcast.5, f32[10,384,128]{2,1,0:T(8,128)} %bitcast.3, f32[10,1,6,128,128]{4,3,2,1,0:T(8,128)} %s_in.1), custom_call_target="tpu_custom_call" | custom-call | flops 8999999488 | bytes 10000000 | tf_op jit(solution)/shard_map/pallas_call | solution.py:330
  76.5 1.3 %copy.6 = f32[10,1,3,128,128]{4,3,2,1,0:T(8,128)} copy(f32[10,1,3,128,128]{4,3,2,1,0:T(8,128)S(1)} %shard_map.46) | data formatting | bytes 3932160

commit v5 on v4

--- a/solution.py
+++ b/solution.py
@@ -239,7 +239,7 @@
             lhs[0, :, n * BS : (n + 1) * BS] = hi
             lhs[1, :, n * BS : (n + 1) * BS] = lo
 
-    def multiply(i, tile, first, last, acc):
+    def multiply(i, tile, first, last, acc, picked=(0, 1)):
         terms = [
             (left, right, n)
             for left, right in ((0, s_hi), (1, s_hi), (0, s_lo))
@@ -255,7 +255,7 @@
                     jnp.concatenate(
                         [
                             right[table[(i * inner + n) * slots + 2 * tile + c]]
-                            for c in range(2)
+                            for c in picked
                         ],
                         axis=1,
                     )
@@ -275,18 +275,21 @@
     def complete(i):
         p_forwarded(i).wait_recv()
         spread(i, direct, inner)
-        for tile in reversed(range(slots // 2)):
-            acc = multiply(i, tile, direct, inner, sums[i, tile])
-            for c in range(2):
+        for tile, picked in ((2, (0, 1)), (1, (1,)), (1, (0,)), (0, (0, 1))):
+            start = picked[0] * BS
+            width = len(picked) * BS
+            before = sums[i, tile, :, start : start + width]
+            acc = multiply(i, tile, direct, inner, before, picked)
+            for at, c in enumerate(picked):
                 slot = 2 * tile + c
-                value = acc[:, c * BS : (c + 1) * BS]
+                value = acc[:, at * BS : (at + 1) * BS]
                 if slot < half:
                     out[i, 0, slot] = value
                 else:
                     part[i, slot - half] = value
-            if tile == 2:
+            if (tile, picked) == (2, (0, 1)):
                 exchange(i, 1, 2).start()
-            if tile == 1:
+            if (tile, picked) == (1, (1,)):
                 exchange(i, 0, 1).start()
 
     @pl.loop(0, rows + 1)

time: 78 us -> 77.9 us (level)
  no operation moved by 1% of the time
where the time goes in v5:
time: 77.9 us; the launch traced here: 77.8 us
  Pallas kernels  76.5 us (98%)
  local copies, waits for them, and re-layouts  1.27 us (2%)
    pallas_call x1, Pallas kernels, per_device(): pl.pallas_call(functools.partial(kernel, (n_row, n_col, rows, half)), out...  76.5 us

profile of v5, /device:TPU:1, one launch (start us, length us, event | category | flops | bytes accessed | tf_op | source)
XLA Modules:
  0.0 77.8 jit_solution(10450374367891943348)
XLA Ops:
  0.0 76.5 %shard_map.46 = f32[10,1,3,128,128]{4,3,2,1,0:T(8,128)S(1)} custom-call(s32[6,4,10]{2,1,0:T(4,128)} %bitcast.4, s32[6,1,160]{2,1,0:T(1,128)} %bitcast.5, f32[10,384,128]{2,1,0:T(8,128)} %bitcast.3, f32[10,1,6,128,128]{4,3,2,1,0:T(8,128)} %s_in.1), custom_call_target="tpu_custom_call" | custom-call | flops 8999999488 | bytes 10000000 | tf_op jit(solution)/shard_map/pallas_call | solution.py:333
  76.5 1.3 %copy.6 = f32[10,1,3,128,128]{4,3,2,1,0:T(8,128)} copy(f32[10,1,3,128,128]{4,3,2,1,0:T(8,128)S(1)} %shard_map.46) | data formatting | bytes 3932160

commit v6 on v4

--- a/solution.py
+++ b/solution.py
@@ -284,10 +284,8 @@
                     out[i, 0, slot] = value
                 else:
                     part[i, slot - half] = value
-            if tile == 2:
-                exchange(i, 1, 2).start()
             if tile == 1:
-                exchange(i, 0, 1).start()
+                exchange(i).start()
 
     @pl.loop(0, rows + 1)
     def _(j):
@@ -314,9 +312,9 @@
         def _():
             finish(j - 2)
 
+    finish(rows - 1)
     for k in range(2):
         p_forward(k, 0, rows).wait_send()
-    finish(rows - 1)
     exchange(0, lines=rows).wait_send()
 
 

time: 78 us -> 78 us (level)
  no operation moved by 1% of the time
where the time goes in v6:
time: 78 us; the launch traced here: 77.8 us
  Pallas kernels  76.5 us (98%)
  local copies, waits for them, and re-layouts  1.27 us (2%)
    pallas_call x1, Pallas kernels, per_device(): pl.pallas_call(functools.partial(kernel, (n_row, n_col, rows, half)), out...  76.5 us

profile of v6, /device:TPU:1, one launch (start us, length us, event | category | flops | bytes accessed | tf_op | source)
XLA Modules:
  0.0 77.8 jit_solution(5970107649468989708)
XLA Ops:
  0.0 76.5 %shard_map.46 = f32[10,1,3,128,128]{4,3,2,1,0:T(8,128)S(1)} custom-call(s32[6,4,10]{2,1,0:T(4,128)} %bitcast.4, s32[6,1,160]{2,1,0:T(1,128)} %bitcast.5, f32[10,384,128]{2,1,0:T(8,128)} %bitcast.3, f32[10,1,6,128,128]{4,3,2,1,0:T(8,128)} %s_in.1), custom_call_target="tpu_custom_call" | custom-call | flops 8999999488 | bytes 10000000 | tf_op jit(solution)/shard_map/pallas_call | solution.py:328
  76.5 1.3 %copy.6 = f32[10,1,3,128,128]{4,3,2,1,0:T(8,128)} copy(f32[10,1,3,128,128]{4,3,2,1,0:T(8,128)S(1)} %shard_map.46) | data formatting | bytes 3932160
